TPU v7x, 32 devices: a whole 2x2x4 slice. The times are simulated.
32 devices in a mesh: stream: 2 (over y), dp: 16 (over z, x, core).
Axes of the slice: x: 2, y: 2, z: 4, core: 2. Of those that a mesh axis runs over, the one named last changes fastest.
Arguments:
- states: bfloat16 [2, 32, 96, 1024], P('stream', 'dp'), may hold values from -6 to 6
- out_grad: bfloat16 [2, 32, 96, 1024], P('stream', 'dp'), may hold values from -6 to 6
- co_params: float32 [2, 8398848], P('stream', 'dp')
- self_params: float32 [2, 7088128], P('stream', 'dp')
- text_lengths: int32 [32], P('dp'), may hold values from 1 to 128, as said below
- region_counts: int32 [32], P('dp'), may hold values from 1 to 96, as said below
Outputs:
- out_states: bfloat16 [2, 32, 96, 1024], P('stream', 'dp')
- states_grad: float32 [2, 32, 96, 1024], P('stream', 'dp')
- co_grad: float32 [2, 8398848], P('stream', 'dp')
- self_grad: float32 [2, 7088128], P('stream', 'dp')
Inputs may be any that keep to these rules, and one draw needn't show every extreme that they name: `text_lengths`: some sequence has exactly 128 text tokens. `region_counts`: some image has exactly 96 regions.
All inputs are finite; a program needn't handle non-finite values.
Results may differ from a plain program's by a relative error of at most 0.02.
Values may be sent and summed in bfloat16 or wider, within the bound.
A program may use at most 320 MiB of HBM per device.

v0:
```python
import functools
import math

import jax
import jax.numpy as jnp
import numpy as np
from jax import lax
from jax.experimental import pallas as pl
from jax.experimental.pallas import tpu as pltpu
from jax.sharding import PartitionSpec as P


MESH_ID = pl.DeviceIdType.MESH
UNITS = 6


def place(line):
    d = lax.axis_index("dp")
    return d // 4, lax.rem(d // 2, 2), lax.rem(d, 2)


F32, BF16 = jnp.float32, jnp.bfloat16
NT = (((1,), (1,)), ((), ()))
TN = (((0,), (0,)), ((), ()))
norm_eps = 1e-12
masked_score = -1000000000.0
other_sequence = -3.0e38


def dot(a, b, dims=(((1,), (0,)), ((), ()))):
    return lax.dot_general(a, b, dims, preferred_element_type=F32)


class Block:
    def __init__(self, width, other, inner, hidden, heads, length, other_length, seqs, base=0):
        self.width, self.other, self.inner, self.hidden, self.heads = width, other, inner, hidden, heads
        self.length, self.other_length, self.seqs = length, other_length, seqs
        self.rows, self.other_rows = length * seqs, other_length * seqs
        self.base = base
        self.place = {}
        self.parts = []
        tile, flat = 0, 0

        def matrix(name, k, n):
            nonlocal tile, flat
            self.place[name] = (tile, k, n)
            self.parts.append((tile, flat, k, k * n // 128, n // 128))
            tile, flat = tile + k * n // 2048, flat + k * n // 128

        def vectors(*names):
            nonlocal tile, flat
            rows = 0
            for name, size in names:
                self.place[name] = (tile, rows, size)
                rows += size // 128
            self.parts.append((tile, flat, 0, rows, 0))
            tile, flat = tile + (rows + 15) // 16, flat + rows

        matrix("q_w", width, inner)
        vectors(("q_b", inner))
        matrix("k_w", other, inner)
        matrix("v_w", other, inner)
        vectors(("v_b", inner))
        matrix("o_w", inner, width)
        vectors(("o_b", width), ("g1", width), ("b1", width))
        matrix("i_w", width, hidden)
        vectors(("i_b", hidden))
        matrix("f_w", hidden, width)
        vectors(("f_b", width), ("g2", width), ("b2", width))
        self.tiles, self.flat_rows = tile, flat


VECS = ("q_b", "v_b", "o_b", "g1", "b1", "i_b", "f_b", "g2", "b2")
GROUPS = (("q_b",), ("v_b",), ("o_b", "g1", "b1"), ("i_b",), ("f_b", "g2", "b2"))


class Cols:
    def __init__(self, j, size):
        self.j, self.size = j, size

    def ds(self):
        return pl.ds(pl.multiple_of(self.j * self.size, self.size), self.size)


def cols(j, size=256):
    return Cols(j, size)


class Pooled:
    def __init__(self, pool, base, rows, width):
        self.pool, self.base, self.rows, self.count = pool, base, rows, width // 128

    def spots(self, index):
        if index is Ellipsis:
            first, count = 0, self.count
        else:
            run = index[1]
            count = run.size // 128
            first = run.j * count
        return [pl.ds(pl.multiple_of(self.base + (first + i) * self.rows, 8), self.rows) for i in range(count)]

    def __getitem__(self, index):
        return jnp.concatenate([self.pool[spot, :] for spot in self.spots(index)], axis=1)

    def __setitem__(self, index, value):
        for i, spot in enumerate(self.spots(index)):
            self.pool[spot, :] = value[:, i * 128 : (i + 1) * 128]


class View:
    def __init__(self, ref, shape):
        self.ref, self.shape = ref, tuple(shape)

    def whole(self, index):
        index = () if index is Ellipsis else index if isinstance(index, tuple) else (index,)
        index = index + (slice(None),) * (len(self.shape) - len(index))
        index = [i.ds() if isinstance(i, Cols) else i for i in index]
        return tuple(slice(0, k) if isinstance(i, slice) and i == slice(None) else i for i, k in zip(index, self.shape))

    def __getitem__(self, index):
        return self.ref[self.whole(index)]

    def __setitem__(self, index, value):
        self.ref[self.whole(index)] = value


NN_STEP, NT_STEP, TN_STEP, TN_WIDE = 1024, 1024, 1024, 768


def step_of(n, most):
    return max(k for k in range(256, most + 1, 256) if n % k == 0)


class Net:
    def __init__(self, b, w, vec, sc):
        self.b, self.w, self.vec, self.s = b, w, vec, sc

    def mat(self, name):
        tile, k, n = self.b.place[name]
        return self.w.at[pl.ds(self.b.base + tile, k * n // 2048)].reshape(k // 16, n // 128, 16, 128)

    def row(self, name, c=None):
        k = VECS.index(name)
        size = self.b.place[name][2]
        return self.vec[k : k + 1, :size] if c is None else self.vec[k : k + 1, c.ds()]

    def load_vectors(self, groups):
        for group in groups:
            tile = self.b.place[group[0]][0]
            rows = sum(self.b.place[g][2] for g in group) // 128
            count = (rows + 15) // 16
            value = self.w[pl.ds(self.b.base + tile, count)].reshape(count * 16, 128).astype(F32)
            r = 0
            for name in group:
                k = VECS.index(name)
                for j in range(self.b.place[name][2] // 128):
                    self.vec[k : k + 1, j * 128 : (j + 1) * 128] = value[r : r + 1]
                    r += 1

    def store_vectors(self, group, scratch):
        tile = self.b.place[group[0]][0]
        rows = sum(self.b.place[g][2] for g in group) // 128
        count = (rows + 15) // 16
        scratch[0 : count * 16] = jnp.zeros((count * 16, 128), F32)
        r = 0
        for name in group:
            k = VECS.index(name)
            for j in range(self.b.place[name][2] // 128):
                scratch[r : r + 1, :] = self.vec[k : k + 1, j * 128 : (j + 1) * 128]
                r += 1
        self.w[pl.ds(self.b.base + tile, count)] = scratch[0 : count * 16].astype(BF16).reshape(count, 16, 128)

    def nn(self, x, name, put):
        m = self.mat(name)
        k, n = self.b.place[name][1:]
        step = step_of(n, NN_STEP)

        def body(j, carry):
            per = step // 128
            w = jnp.concatenate([m[:, per * j + i].reshape(k, 128) for i in range(per)], axis=1)
            put(cols(j, step), dot(x[...], w))
            return carry

        lax.fori_loop(0, n // step, body, 0)

    def rows_of(self, name, j, step):
        m = self.mat(name)
        strips = step // 16
        return jnp.concatenate([m[pl.ds(j * strips, strips), i].reshape(step, 128) for i in range(m.shape[1])], axis=1)

    def nt(self, g, name, put):
        k, n = self.b.place[name][1:]
        step = step_of(k, NT_STEP)

        def body(j, carry):
            put(cols(j, step), dot(g[...], self.rows_of(name, j, step), NT))
            return carry

        lax.fori_loop(0, k // step, body, 0)

    def tn(self, a, g, name):
        m = self.mat(name)
        k, n = self.b.place[name][1:]
        step, wide = step_of(k, TN_STEP), step_of(n, TN_WIDE)
        strips = step // 16

        def body(j, carry):
            left = a[:, cols(j, step)].T
            for i in range(n // wide):
                got = dot(left, g[:, cols(i, wide)]).astype(BF16)
                for c in range(wide // 128):
                    m[pl.ds(j * strips, strips), i * (wide // 128) + c] = got[:, c * 128 : (c + 1) * 128].reshape(strips, 16, 128)
            return carry

        lax.fori_loop(0, k // step, body, 0)

    def norm(self, r, gain, shift):
        centre = r - jnp.mean(r, axis=-1, keepdims=True)
        spread = jnp.mean(centre * centre, axis=-1, keepdims=True)
        return centre * lax.rsqrt(spread + norm_eps) * self.row(gain) + self.row(shift)

    def norm_back(self, r, dy, gain, shift):
        centre = r - jnp.mean(r, axis=-1, keepdims=True)
        spread = jnp.mean(centre * centre, axis=-1, keepdims=True)
        s = lax.rsqrt(spread + norm_eps)
        xh = centre * s
        t = dy * self.row(gain)
        dr = s * (t - jnp.mean(t, axis=-1, keepdims=True) - xh * jnp.mean(t * xh, axis=-1, keepdims=True))
        size = self.b.width
        kg, kb = VECS.index(gain), VECS.index(shift)
        self.vec[kg : kg + 1, :size] = jnp.sum(dy * xh, axis=0, keepdims=True)
        self.vec[kb : kb + 1, :size] = jnp.sum(dy, axis=0, keepdims=True)
        return dr

    def put_sum(self, name, ref):
        k = VECS.index(name)
        self.vec[k : k + 1, : self.b.place[name][2]] = jnp.sum(ref[...].astype(F32), axis=0, keepdims=True)

    def mask(self, fill, counts):
        b = self.b
        shape = (b.rows, b.other_rows)
        row = lax.broadcasted_iota(jnp.int32, shape, 0)
        col = lax.broadcasted_iota(jnp.int32, shape, 1)
        value = jnp.full(shape, other_sequence, F32)
        for q in range(b.seqs):
            mine = (row >= q * b.length) & (row < (q + 1) * b.length)
            mine = mine & (col >= q * b.other_length) & (col < (q + 1) * b.other_length)
            value = jnp.where(mine, jnp.where(col < q * b.other_length + counts(q), 1.0, masked_score), value)
        fill[...] = value

    def heads_of(self, refs, g):
        e = self.b.inner // self.b.heads
        values = [ref[:, cols(g, 128)] for ref in refs]
        if e == 128:
            return [values]
        lane = lax.broadcasted_iota(jnp.int32, (1, 128), 1)
        return [
            [jnp.where((lane >= h * e) & (lane < (h + 1) * e), value, jnp.zeros((), BF16)) for value in values]
            for h in range(128 // e)]

    def attend(self, q, k, v, fill, p, c):
        b = self.b
        e = b.inner // b.heads
        scale = 1.0 / math.sqrt(e)
        per = max(128 // e, 1)

        def body(g, carry):
            keys = k[:, cols(g, 128)]
            total = None
            for h, (qh,) in enumerate(self.heads_of([q], g)):
                vh = self.heads_of([v], g)[h][0]
                s = dot(qh, keys, NT) * scale
                f = fill[...]
                s = jnp.where(f > 0, s, f)
                ex = jnp.exp(s - jnp.max(s, axis=-1, keepdims=True))
                probs = (ex * (1.0 / jnp.sum(ex, axis=-1, keepdims=True))).astype(BF16)
                p[g * per + h] = probs
                got = dot(probs, vh)
                total = got if total is None else total + got
            c[:, cols(g, 128)] = total.astype(BF16)
            return carry

        lax.fori_loop(0, b.inner // 128, body, 0, unroll=True)

    def attend_back(self, q, k, v, p, dc):
        b = self.b
        e = b.inner // b.heads
        scale = 1.0 / math.sqrt(e)
        per = max(128 // e, 1)

        def body(g, carry):
            values = v[:, cols(g, 128)]
            sums = None
            for h, (qh, kh, dh) in enumerate(self.heads_of([q, k, dc], g)):
                probs = p[g * per + h]
                dp = dot(dh, values, NT)
                wide = probs.astype(F32)
                ds = (wide * (dp - jnp.sum(wide * dp, axis=-1, keepdims=True))).astype(BF16)
                got = [dot(ds, kh), dot(ds, qh, TN), dot(probs, dh, TN)]
                sums = got if sums is None else [x + y for x, y in zip(sums, got)]
            q[:, cols(g, 128)] = (sums[0] * scale).astype(BF16)
            k[:, cols(g, 128)] = (sums[1] * scale).astype(BF16)
            v[:, cols(g, 128)] = sums[2].astype(BF16)
            return carry

        lax.fori_loop(0, b.inner // 128, body, 0, unroll=True)

    def forward(self, x, u, z, counts, tick=lambda k=1: None, need=lambda name: None):
        s, b = self.s, self.b
        need("o_w")
        self.load_vectors(GROUPS[:3])
        self.mask(s["fill"], counts)

        def put(ref, bias=None):
            def store(c, value):
                if bias is not None:
                    value = value + self.row(bias, c)
                ref[:, c] = value.astype(BF16)
            return store

        tick()
        self.nn(u, "q_w", put(s["q"], "q_b"))
        self.nn(z, "k_w", put(s["k"]))
        tick()
        self.nn(z, "v_w", put(s["v"], "v_b"))
        tick()
        self.attend(s["q"], s["k"], s["v"], s["fill"], s["p"], s["c"])

        tick()

        def first(c, value):
            s["r1"][:, c] = x[:, c].astype(F32) + (value + self.row("o_b", c))

        self.nn(s["c"], "o_w", first)
        y1 = self.norm(s["r1"][...], "g1", "b1")
        s["r2"][...] = y1
        s["y1"][...] = y1.astype(BF16)

        def up(c, value):
            value = value + self.row("i_b", c)
            half = 0.5 * (1.0 + lax.erf(value * (1.0 / math.sqrt(2.0))))
            s["a"][:, c] = (value * half).astype(BF16)
            s["gp"][:, c] = (half + value * (jnp.exp(-0.5 * value * value) * (1.0 / math.sqrt(2.0 * math.pi)))).astype(BF16)

        tick()
        need("i_w")
        self.load_vectors(GROUPS[3:4])
        self.nn(s["y1"], "i_w", up)
        tick()
        need("f_w")
        self.load_vectors(GROUPS[4:])

        def second(c, value):
            s["r2"][:, c] = s["r2"][:, c] + (value + self.row("f_b", c))

        self.nn(s["a"], "f_w", second)
        return self.norm(s["r2"][...], "g2", "b2")

    def backward(self, dy, u, z, put_resid, put_z, done, tick=lambda k=1: None):
        s, b = self.s, self.b
        small = s["small"]
        dr2 = self.norm_back(s["r2"][...], dy[...], "g2", "b2")
        dy[...] = dr2
        s["m"][...] = dr2.astype(BF16)
        self.put_sum("f_b", s["m"])

        def inner(c, value):
            s["gp"][:, c] = (value * s["gp"][:, c].astype(F32)).astype(BF16)

        self.nt(s["m"], "f_w", inner)
        self.store_vectors(GROUPS[4], small)
        self.tn(s["a"], s["m"], "f_w")
        done("f_w")
        tick()
        self.put_sum("i_b", s["gp"])

        def mid(c, value):
            dy[:, c] = dy[:, c] + value

        self.nt(s["gp"], "i_w", mid)
        tick()
        self.store_vectors(GROUPS[3], small)
        self.tn(s["y1"], s["gp"], "i_w")
        done("i_w")
        tick()
        dr1 = self.norm_back(s["r1"][...], dy[...], "g1", "b1")
        dy[...] = dr1
        s["m"][...] = dr1.astype(BF16)
        self.put_sum("o_b", s["m"])

        def context(c, value):
            s["dc"][:, c] = value.astype(BF16)

        self.nt(s["m"], "o_w", context)
        self.store_vectors(GROUPS[2], small)
        self.tn(s["c"], s["m"], "o_w")
        done("o_w")
        tick(2)
        self.attend_back(s["q"], s["k"], s["v"], s["p"], s["dc"])

        tick(2)

        def resid(c, value):
            put_resid(c, dy[:, c] + value)

        self.nt(s["q"], "q_w", resid)
        k = b.place["v_w"][1]
        step = step_of(k, NT_STEP)

        def body(j, carry):
            value = dot(s["k"][...], self.rows_of("k_w", j, step), NT) + dot(s["v"][...], self.rows_of("v_w", j, step), NT)
            put_z(cols(j, step), value)
            return carry

        lax.fori_loop(0, k // step, body, 0)
        tick()
        self.put_sum("q_b", s["q"])
        self.put_sum("v_b", s["v"])
        self.store_vectors(GROUPS[0], small)
        self.store_vectors(GROUPS[1], small)
        self.tn(u, s["q"], "q_w")
        self.tn(z, s["k"], "k_w")
        self.tn(z, s["v"], "v_w")
        done("q_w")
        tick()


def scratch_of(b):
    return {
        "q": ((b.rows, b.inner), BF16), "k": ((b.other_rows, b.inner), BF16), "v": ((b.other_rows, b.inner), BF16),
        "p": ((b.heads, b.rows, b.other_rows), BF16), "c": ((b.rows, b.inner), BF16),
        "r1": ((b.rows, b.width), F32), "r2": ((b.rows, b.width), F32), "y1": ((b.rows, b.width), BF16),
        "a": ((b.rows, b.hidden), BF16), "gp": ((b.rows, b.hidden), BF16), "fill": ((b.rows, b.other_rows), F32)}


def compute_kernel(co, sa, lens, x, xp, gy, wco, wsa, out, own_grad, sent, gco, gsa, wc, ws, vec, vec2, small, sems, *scr):
    names = sorted(scratch_of(co))
    sc = dict(zip(names, scr[: len(names)]))
    ss = dict(zip(names, scr[len(names) : 2 * len(names)]))
    rest = scr[2 * len(names) :]
    m, dy, h, hb, dcc, dcs = rest
    for d, dc in ((sc, dcc), (ss, dcs)):
        d["m"], d["small"], d["dc"] = m, small, dc
    x, xp = View(x, (co.rows, co.width)), View(xp, (co.other_rows, co.other))
    own_grad, sent = View(own_grad, (co.rows, co.width)), View(sent, (co.other_rows, co.other))
    h, hb, dy = [View(r, (co.rows, co.width)) for r in (h, hb, dy)]
    for b, d in ((co, sc), (sa, ss)):
        shapes = {**{n: k[0] for n, k in scratch_of(b).items()}, "m": (b.rows, b.width), "dc": (b.rows, b.inner)}
        for n, shape in shapes.items():
            d[n] = View(d[n], shape)
    copies = [pltpu.make_async_copy(wco, wc, sems.at[0]), pltpu.make_async_copy(wsa, ws, sems.at[1])]
    for cp in copies:
        cp.start()
    copies[0].wait()
    a = Net(co, wc, vec, sc)
    bnet = Net(sa, ws, vec2, ss)
    value = a.forward(x, x, xp, lambda q: lens[1, q])
    h[...] = value
    hb[...] = value.astype(BF16)
    copies[1].wait()
    out[...] = bnet.forward(h, hb, hb, lambda q: lens[0, q]).astype(BF16)
    dy[...] = gy[...].astype(F32)

    def put_h(c, value):
        h[:, c] = value

    def add_h(c, value):
        h[:, c] = h[:, c] + value

    bnet.backward(dy, hb, hb, put_h, add_h, lambda name: None)
    back = pltpu.make_async_copy(ws, gsa, sems.at[1])
    back.start()

    def put_own(c, value):
        own_grad[:, c] = value

    def put_sent(c, value):
        sent[:, c] = value.astype(BF16)

    a.backward(h, x, xp, put_own, put_sent, lambda name: None)
    back2 = pltpu.make_async_copy(wc, gco, sems.at[0])
    back2.start()
    back.wait()
    back2.wait()


def compute(co, sa, lens, x, xp, gy, wco, wsa):
    any_ = pl.BlockSpec(memory_space=pl.ANY)
    vm = pl.BlockSpec(memory_space=pltpu.VMEM)
    names = sorted(scratch_of(co))
    V = lambda shape, dtype: pltpu.VMEM(shape, dtype)
    scr = [V(wco.shape, BF16), V(wsa.shape, BF16), V((16, 3072), F32), V((16, 3072), F32), V((32, 128), F32), pltpu.SemaphoreType.DMA((2,))]
    scr += [V(*scratch_of(co)[n]) for n in names] + [V(*scratch_of(sa)[n]) for n in names]
    rows, width = co.rows, co.width
    scr += [V((rows, width), BF16), V((rows, width), F32), V((rows, width), F32), V((rows, width), BF16)]
    scr += [V((b.rows, b.inner), BF16) for b in (co, sa)]
    return pl.pallas_call(
        functools.partial(compute_kernel, co, sa),
        out_shape=(jax.ShapeDtypeStruct((rows, width), BF16), jax.ShapeDtypeStruct((rows, width), F32),
                   jax.ShapeDtypeStruct((co.other_rows, co.other), BF16),
                   jax.ShapeDtypeStruct(wco.shape, BF16), jax.ShapeDtypeStruct(wsa.shape, BF16)),
        in_specs=[pl.BlockSpec(memory_space=pltpu.SMEM), vm, vm, vm, any_, any_],
        out_specs=(vm, vm, vm, any_, any_),
        scratch_shapes=scr,
        compiler_params=pltpu.CompilerParams(vmem_limit_bytes=63 * 2**20),
        name="compute",
    )(lens, x, xp, gy, wco, wsa)


PER = UNITS + 1
BEHIND = 4
LEAD = 3


class Where:
    def __init__(self, line):
        self.line, self.last = line, line - 1
        self.z, self.x, self.c = place(line)
        self.s = lax.axis_index("stream")

    def copy(self, src, dst, send, recv, z, x, c, s=None):
        return pltpu.make_async_remote_copy(
            src_ref=src, dst_ref=dst, send_sem=send, recv_sem=recv,
            device_id=(self.s if s is None else s, (z * 2 + x) * 2 + c), device_id_type=MESH_ID)

    def greet(self):
        z, x, c, s = self.z, self.x, self.c, self.s
        barrier = pltpu.get_barrier_semaphore()

        def signal(zz, xx, cc, ss):
            pl.semaphore_signal(barrier, inc=1, device_id=(ss, (zz * 2 + xx) * 2 + cc), device_id_type=MESH_ID)

        signal(z, 1 - x, c, s)
        signal(z, x, 1 - c, s)
        signal(z, x, c, 1 - s)
        d = (z * 2 + x) * 2 + c
        beside = (1 - c) * jnp.minimum(d, 1) + c * jnp.minimum(4 * self.line - 1 - d, 1)

        @pl.when(beside > 0)
        def _():
            pl.semaphore_signal(barrier, inc=1, device_id=(s, d - 1 + 2 * c), device_id_type=MESH_ID)

        @pl.when(z > 0)
        def _():
            signal(z - 1, x, c, s)

        @pl.when(z < self.last)
        def _():
            signal(z + 1, x, c, s)

        pl.semaphore_wait(barrier, 3 + jnp.minimum(z, 1) + jnp.minimum(self.last - z, 1) + beside)


class Gather:
    def __init__(self, at, rows, w, sems):
        self.at, self.rows, self.w = at, rows, w
        self.n = self.rows // UNITS
        self.up_s, self.dn_s, self.z_r, self.x_s, self.x_r, self.c_s, self.c_r, self.o_s = sems

    def spot(self, zo, xb, cc, u):
        return self.w.at[pl.ds(((zo * 2 + xb) * 2 + cc) * self.rows + u * self.n, self.n)]

    def block_of(self, v):
        x = self.at.x
        return jnp.where(v == UNITS, 1 - x, x), jnp.minimum(v, UNITS - 1)

    def z_copy(self, zo, v, up):
        at = self.at
        xb, u = self.block_of(v)
        spot = self.spot(zo, xb, at.c, u)
        return at.copy(spot, spot, (self.up_s if up else self.dn_s).at[zo], self.z_r.at[zo * PER + v], at.z + 1 if up else at.z - 1, at.x, at.c)

    def x_copy(self, zo, u, arriving=False, first=False):
        at = self.at
        spot = self.spot(zo, 1 - at.x if arriving else at.x, at.c, u)
        return at.copy(spot, spot, self.o_s if first else self.x_s.at[zo], self.x_r.at[zo * UNITS + u], at.z, 1 - at.x, at.c)

    def c_copy(self, zo, xb, u):
        at = self.at
        spot = self.spot(zo, xb, at.c, u)
        return at.copy(spot, spot, self.c_s.at[zo], self.c_r.at[zo], at.z, at.x, 1 - at.c)

    def send_z(self, zo, v, up):
        at = self.at

        @pl.when(at.z < at.last if up else at.z > 0)
        def _():
            self.z_copy(zo, v, up).start()

    def first(self):
        self.x_copy(self.at.z, UNITS - 1, first=True).start()

    def start(self, up):
        at = self.at
        z, x = at.z, at.x
        for u in range(UNITS - 1):
            self.x_copy(z, u).start()
            self.send_z(z, u, False)
            if up:
                self.send_z(z, u, True)
        self.send_z(z, UNITS - 1, False)
        if up:
            self.send_z(z, UNITS - 1, True)
        for u in range(UNITS):
            self.c_copy(z, x, u).start()

    def other_last(self, up):
        at = self.at
        self.x_copy(at.z, UNITS - 1, arriving=True).wait_recv()
        self.send_z(at.z, UNITS, False)
        if up:
            self.send_z(at.z, UNITS, True)
        self.c_copy(at.z, 1 - at.x, UNITS - 1).start()

    def onward(self, zo, v, up):
        xb, u = self.block_of(v)
        self.z_copy(zo, v, up).wait_recv()
        self.send_z(zo, v, up)

        @pl.when(v < UNITS - 1)
        def _():
            self.x_copy(zo, u).start()

        self.c_copy(zo, xb, u).start()

    def from_below(self, t):
        h, v = t // PER, lax.rem(t, PER)

        @pl.when(self.at.z > h)
        def _():
            self.onward(self.at.z - 1 - h, v, True)

    def from_above(self, t):
        h, v = t // PER, lax.rem(t, PER)

        @pl.when(self.at.z + h < self.at.last)
        def _():
            self.onward(self.at.z + 1 + h, v, False)

    def in_order(self, i):
        z = self.at.z
        zo, v = i // PER, lax.rem(i, PER)

        @pl.when(jnp.logical_and(i >= 0, zo < z))
        def _():
            self.onward(zo, v, True)

        @pl.when(jnp.logical_and(i >= 0, zo == z))
        def _():
            self.send_z(z, v, True)

    def x_arrival(self, zo, u):
        self.x_copy(zo, u, arriving=True).wait_recv()
        self.c_copy(zo, 1 - self.at.x, u).start()

    def beside_own(self):
        for u in range(UNITS - 1):
            self.x_arrival(self.at.z, u)

    def beside_far(self, t):
        at = self.at
        h, v = t // PER, lax.rem(t, PER)

        @pl.when(jnp.logical_and(t >= 0, v < UNITS - 1))
        def _():
            @pl.when(at.z > h)
            def _():
                self.x_arrival(at.z - 1 - h, v)

            @pl.when(at.z + h < at.last)
            def _():
                self.x_arrival(at.z + 1 + h, v)

    def beside_order(self, i):
        zo, v = i // PER, lax.rem(i, PER)

        @pl.when(jnp.logical_and(jnp.logical_and(i >= 0, v < UNITS - 1), zo < self.at.z))
        def _():
            self.x_arrival(zo, v)

    def beside_above(self, t):
        at = self.at
        h, v = t // PER, lax.rem(t, PER)

        @pl.when(jnp.logical_and(jnp.logical_and(t >= 0, v < UNITS - 1), at.z + h < at.last))
        def _():
            self.x_arrival(at.z + 1 + h, v)

    def arrived(self, zo):
        at = self.at
        spot = self.w.at[pl.ds(0, 2 * self.rows)]
        at.copy(spot, spot, self.o_s, self.c_r.at[zo], at.z, at.x, 1 - at.c).wait_recv()

    def sent(self):
        at = self.at
        z = at.z

        def wait(tiles, sem):
            spot = self.w.at[pl.ds(0, tiles)]
            at.copy(spot, spot, sem, self.c_r.at[0], z, at.x, 1 - at.c).wait_send()

        def each(zo, carry):
            @pl.when(jnp.logical_and(z < at.last, zo <= z))
            def _():
                wait(PER * self.n, self.up_s.at[zo])

            @pl.when(jnp.logical_and(z > 0, zo >= z))
            def _():
                wait(PER * self.n, self.dn_s.at[zo])

            wait((UNITS - 1) * self.n, self.x_s.at[zo])
            wait(2 * self.rows, self.c_s.at[zo])
            return carry

        lax.fori_loop(0, at.line, each, 0)
        wait(self.n, self.o_s)


def gather_sems(line):
    dma = pltpu.SemaphoreType.DMA
    return [dma((line,)), dma((line,)), dma((line * PER,)), dma((line,)), dma((line * UNITS,)), dma((line,)), dma((line,)), dma]


class Scatter:
    def __init__(self, at, g, rows, cr, xr, zr, keep, stage, wide_stage, behind, sems):
        self.at, self.g, self.rows, self.n = at, g, rows, rows // UNITS
        self.cr, self.xr, self.zr, self.keep, self.stage, self.wide = cr, xr, zr, keep, stage, wide_stage
        self.c_s, self.c_r, self.x_s, self.x_r, self.z_s, self.z_r, self.l_s, self.b_s = sems
        self.behind = behind
        self.items = at.last * PER
        self.final = self.items + LEAD + at.last + behind
        self.slots = self.final + PER

    def mine(self, zo, xb, u):
        return pl.ds(((zo * 2 + xb) * 2 + self.at.c) * self.rows + u * self.n, self.n)

    def block_of(self, v):
        x = self.at.x
        return jnp.where(v == 0, 1 - x, x), jnp.where(v == 0, UNITS - 1, v - 1)

    def c_copy(self, zo, xb):
        at = self.at
        src = self.g.at[pl.ds(((zo * 2 + xb) * 2 + 1 - at.c) * self.rows, self.rows)]
        k = zo * 2 + xb
        return at.copy(src, self.cr.at[k], self.c_s.at[zo], self.c_r.at[k], at.z, at.x, 1 - at.c)

    def x_copy(self, zo, u, last=False):
        at = self.at
        k = zo * UNITS + u
        return at.copy(self.g.at[self.mine(zo, 1 - at.x, u)], self.xr.at[k], self.b_s if last else self.x_s.at[zo], self.x_r.at[k],
                       at.z, 1 - at.x, at.c)

    def z_copy(self, to, v, up):
        at = self.at
        xb, u = self.block_of(v)
        there = at.z + 1 if up else at.z - 1
        k = (to if up else jnp.where(to == there, at.line, to)) * PER + v
        return at.copy(self.g.at[self.mine(to, xb, u)], self.zr.at[k], self.z_s.at[to], self.z_r.at[k], there, at.x, at.c)

    def z_wait(self, k):
        at = self.at
        spot = self.zr.at[k]
        at.copy(spot, spot, self.z_s.at[0], self.z_r.at[k], at.z, 1 - at.x, at.c).wait_recv()

    def ready(self, zo):
        for xb in range(2):
            self.c_copy(zo, xb).start()

    def load(self, src, slot):
        return pltpu.make_async_copy(src, self.stage.at[slot, pl.ds(0, self.n)], self.l_s.at[slot])

    def core_part(self, zo, xb, u):
        return self.cr.at[zo * 2 + xb, pl.ds(u * self.n, self.n)]

    def way(self, t, up):
        at = self.at
        i = t - (at.z if up else at.last - at.z + self.behind)
        to = (at.last if up else at.last - 1) - i // PER
        here = jnp.logical_and(jnp.logical_and(i >= 0, i < self.items), to > at.z if up else to < at.z)
        return to, lax.rem(i, PER), here

    def crossings(self, t):
        at = self.at
        found = []
        for up, slot in ((True, 0), (False, 11)):
            to, v, here = self.way(t, up)
            found.append((to, v - 1, jnp.logical_and(here, jnp.logical_and(v >= 1, v < UNITS)), slot))
        u = t - self.items - self.behind - 1
        found.append((at.z, u, jnp.logical_and(u >= 0, u < UNITS - 1), 0))
        return found

    def parts(self, t, finals):
        found = [self.way(t - LEAD, up) + (up, slot) for up, slot in ((True, 1), (False, 4))]
        own = t - self.final
        return found + [(self.at.z, own, jnp.logical_and(own >= 0, own < PER), None, 7)] * finals

    def prepare(self, t, finals=False):
        at = self.at
        for to, u, here, slot in self.crossings(t):
            @pl.when(here)
            def _(to=to, u=u, slot=slot):
                @pl.when(u == 0)
                def _():
                    for xb in range(2):
                        self.c_copy(to, xb).wait_recv()

                self.load(self.core_part(to, 1 - at.x, u), slot).start()

        for to, v, here, up, slot in self.parts(t, finals):
            @pl.when(here)
            def _(to=to, v=v, up=up, slot=slot):
                xb, u = self.block_of(v)
                self.load(self.core_part(to, xb, u), slot).start()

                @pl.when(jnp.logical_and(v >= 1, v < (UNITS if up is not None else PER)))
                def _():
                    self.x_copy(to, u).wait_recv()
                    self.load(self.xr.at[to * UNITS + u], slot + 1).start()

                if up is None:
                    @pl.when(at.z > 0)
                    def _():
                        self.z_wait(to * PER + v)
                        self.load(self.zr.at[to * PER + v], slot + 2).start()

                    @pl.when(at.z < at.last)
                    def _():
                        self.z_wait(at.line * PER + v)
                        self.load(self.zr.at[at.line * PER + v], slot + 3).start()
                else:
                    @pl.when(at.z != (0 if up else at.last))
                    def _():
                        self.z_wait(to * PER + v)
                        self.load(self.zr.at[to * PER + v], slot + 2).start()

    def take(self, slot):
        self.load(self.xr.at[0], slot).wait()
        return self.stage[slot].astype(F32)

    def act(self, t, finals):
        at = self.at
        for to, v, here, up, slot in self.parts(t, finals):
            @pl.when(here)
            def _(to=to, v=v, up=up, slot=slot):
                xb, u = self.block_of(v)
                spot = self.mine(to, xb, u)
                acc = self.wide

                acc[: self.n] = self.g[spot].astype(F32) + self.take(slot)

                def more(k):
                    acc[: self.n] = acc[: self.n] + self.take(slot + k)

                @pl.when(jnp.logical_and(v >= 1, v < (UNITS if up is not None else PER)))
                def _():
                    more(1)

                if up is None:
                    @pl.when(at.z > 0)
                    def _():
                        more(2)

                    @pl.when(at.z < at.last)
                    def _():
                        more(3)

                    @pl.when(v == 0)
                    def _():
                        self.g[spot] = acc[: self.n].astype(BF16)
                        self.x_copy(to, UNITS - 1, True).start()

                    @pl.when(v >= 1)
                    def _():
                        self.keep(u)
                else:
                    @pl.when(at.z != (0 if up else at.last))
                    def _():
                        more(2)

                    self.g[spot] = acc[: self.n].astype(BF16)
                    self.z_copy(to, v, up).start()

        for to, u, here, slot in self.crossings(t):
            @pl.when(here)
            def _(to=to, u=u, slot=slot):
                spot = self.mine(to, 1 - at.x, u)
                self.g[spot] = (self.g[spot].astype(F32) + self.take(slot)).astype(BF16)
                self.x_copy(to, u).start()

    def slot(self, t, finals=False):
        self.act(t, finals)
        self.prepare(t + 1, finals)

    def sent(self):
        at = self.at
        z = at.z

        def wait(tiles, sem):
            spot = self.g.at[pl.ds(0, tiles)]
            at.copy(spot, spot, sem, self.c_r.at[0], z, at.x, 1 - at.c).wait_send()

        def each(zo, carry):
            @pl.when(zo != z)
            def _():
                wait(PER * self.n, self.z_s.at[zo])

            wait((UNITS - 1) * self.n, self.x_s.at[zo])
            wait(2 * self.rows, self.c_s.at[zo])
            return carry

        lax.fori_loop(0, at.line, each, 0)
        wait(self.n, self.b_s)


def scatter_sems(line):
    dma = pltpu.SemaphoreType.DMA
    return [dma((line,)), dma((line * 2,)), dma((line,)), dma((line * UNITS,)), dma((line,)), dma(((line + 1) * PER,)), dma((12,)), dma]


def landing(line, rows):
    n = rows // UNITS
    shape = lambda *s: jax.ShapeDtypeStruct(s + (16, 128), BF16)
    return [shape(line * 2, rows), shape(line * UNITS, n), shape((line + 1) * PER, n)]


class Edges:
    def __init__(self, at, plan, window, first, spare, land, sems):
        self.at, self.plan, self.window, self.first, self.spare, self.land = at, plan, window, first, spare, land
        self.f_s, self.f_r, self.l_s, self.e_s, self.e_r = sems
        self.d = (at.z * 2 + at.x) * 2 + at.c
        self.end = plan.before + plan.shard

    def over(self, src, dst, send, recv, by):
        return pltpu.make_async_remote_copy(
            src_ref=src, dst_ref=dst, send_sem=send, recv_sem=recv, device_id=(self.at.s, self.d + by), device_id_type=MESH_ID)

    def both(self, up, down):
        @pl.when(self.d < 4 * self.at.line - 1)
        def _():
            up()

        @pl.when(self.d > 0)
        def _():
            down()

    def lands(self, ref):
        plan = self.plan
        return ref.at[pl.ds(0, plan.before)], ref.at[pl.ds(plan.before, plan.after)]

    def outer(self, own):
        plan = self.plan
        before, after = self.lands(self.first)
        return (self.over(own.at[pl.ds(plan.shard - plan.before, plan.before), 0], before, self.f_s.at[0], self.f_r.at[0], 1),
                self.over(own.at[pl.ds(0, plan.after), 0], after, self.f_s.at[1], self.f_r.at[1], -1))

    def send(self, own):
        up, down = self.outer(own)
        self.both(up.start, down.start)

    def inner(self, own):
        return pltpu.make_async_copy(own.at[:, 0], self.window.at[pl.ds(self.plan.before, self.plan.shard)], self.l_s)

    def tiles(self, kinds, own, w):
        plan = self.plan
        up, down = self.outer(own)
        lo = plan.rows * self.d
        w[pl.ds(lo, plan.rows)] = jnp.zeros((plan.rows, 16, 128), w.dtype)

        def above():
            down.wait_recv()
            self.window[self.end : self.end + plan.after, :] = self.first[plan.before : plan.before + plan.after, :]

        def below():
            up.wait_recv()
            self.window[: plan.before, :] = self.first[: plan.before, :]

        self.both(above, below)
        self.inner(own).wait()

        def act(tile, row, stride, rows):
            value = self.window[pl.ds(row, rows, stride=stride), :]
            if rows < 16:
                value = jnp.concatenate([value, jnp.zeros((16 - rows, 128), value.dtype)], axis=0)
            w[tile] = value.astype(w.dtype)

        self.by_stream(kinds, lo, lo + plan.rows, act)
        self.both(up.wait_send, down.wait_send)

    def by_stream(self, kinds, lo, hi, act):
        start = self.plan.shard * self.d - self.plan.before
        for s, b in enumerate(kinds):
            @pl.when(self.at.s == s)
            def _(b=b):
                each_tile(b, lo, hi, start, act)

    def clear(self):
        self.window[...] = jnp.zeros(self.window.shape, F32)

    def take(self, kinds, acc, n):
        def keep(u):
            lo = self.plan.rows * self.d + u * n

            def act(tile, row, stride, rows):
                self.window[pl.ds(row, rows, stride=stride), :] = acc[tile - lo][:rows]

            self.by_stream(kinds, lo, lo + n, act)

        return keep

    def back(self):
        plan = self.plan
        front, rear = self.lands(self.land)
        return (self.over(self.spare.at[pl.ds(0, plan.after)], rear, self.e_s.at[0], self.e_r.at[0], 1),
                self.over(self.window.at[pl.ds(0, plan.before)], front, self.e_s.at[1], self.e_r.at[1], -1))

    def give(self):
        self.spare[: self.plan.after, :] = self.window[self.end : self.end + self.plan.after, :]
        up, down = self.back()
        self.both(up.start, down.start)

    def finish(self, out):
        plan = self.plan
        up, down = self.back()

        def above():
            down.wait_recv()
            spot = slice(self.end - plan.before, self.end)
            self.window[spot, :] = self.window[spot, :] + self.land[: plan.before, :]

        def below():
            up.wait_recv()
            spot = slice(plan.before, plan.before + plan.after)
            self.window[spot, :] = self.window[spot, :] + self.land[plan.before : plan.before + plan.after, :]

        self.both(above, below)
        self.leave(out).start()

    def leave(self, out):
        return pltpu.make_async_copy(self.window.at[pl.ds(self.plan.before, self.plan.shard)], out.at[:, 0], self.l_s)

    def done(self, out):
        self.leave(out).wait()
        up, down = self.back()
        self.both(up.wait_send, down.wait_send)


def edge_sems():
    dma = pltpu.SemaphoreType.DMA
    return [dma((2,)), dma((2,)), dma, dma((2,)), dma((2,))]


def to_flat(flat, box):
    count = box.shape[1] // 128
    for b in range(count):
        flat[pl.ds(b, box.shape[0], stride=count), :] = box[:, b * 128 : (b + 1) * 128].astype(F32)


def from_flat(flat, rows, count, put):
    for j in range(count):
        put(j, flat[pl.ds(j, rows, stride=count), :])


def layer_kernel(plans, line, lens, xbox, gbox, co_flat, sa_flat, *refs):
    kinds = list(zip(plans[0].blocks, plans[1].blocks))
    outs, refs = refs[:10], refs[10:]
    out_box, grad_box, co_out, sa_out = outs[:4]
    wc, ws, vec, vec2, small, pool, land, xp, xin, ret, stage_c, stage_s, acc = refs[:13]
    refs = refs[13:]
    names = sorted(KEPT)
    sc = dict(zip(names, refs[: len(names)]))
    refs = refs[len(names) :]
    ss = dict(zip(names, refs[: len(names)]))
    refs = refs[len(names) :]
    shared = dict(zip(sorted(SHARED), refs[: len(SHARED)]))
    refs = refs[len(SHARED) :]
    ag_c, ag_s, rs_c, rs_s, ed_c, ed_s, y_s, y_r = refs[:8], refs[8:16], refs[16:24], refs[24:32], refs[32:37], refs[37:42], refs[42], refs[43]
    sent = shared["dc"]
    span = pool_span(plans)
    flat = pool.at[pl.ds(6 * span, span)]

    at = Where(line)
    last = at.last
    gc, gs = Gather(at, plans[0].rows, wc, ag_c), Gather(at, plans[1].rows, ws, ag_s)
    edges = []
    rest = max(p.window for p in plans)
    for k, (p, sems) in enumerate(zip(plans, (ed_c, ed_s))):
        sizes = [q.before + q.after for q in plans]
        edges.append(Edges(at, p, pool.at[pl.ds(0, p.window)], pool.at[pl.ds(rest + k * sizes[0], sizes[k])], pool.at[pl.ds(rest, p.after)],
                           land.at[pl.ds(k * sizes[0], sizes[k])], sems))
    ec, es = edges
    own_kinds = [[k[i] for k in kinds] for i in range(2)]
    rc = Scatter(at, wc, plans[0].rows, *outs[4:7], ec.take(own_kinds[0], acc, gc.n), stage_c, acc, 0, rs_c)
    rs = Scatter(at, ws, plans[1].rows, *outs[7:10], es.take(own_kinds[1], acc, gs.n), stage_s, acc, BEHIND, rs_s)

    def over(k, src, dst):
        return at.copy(src, dst, y_s.at[k], y_r.at[k], at.z, at.x, at.c, 1 - at.s)

    ec.inner(co_flat).start()
    at.greet()
    ec.send(co_flat)
    es.send(sa_flat)
    ec.tiles(own_kinds[0], co_flat, wc)
    gc.first()
    gc.start(True)
    es.inner(sa_flat).start()
    states = over(0, xbox, xp)
    states.start()
    es.tiles(own_kinds[1], sa_flat, ws)
    gs.first()
    gc.other_last(True)

    steps = PER * last
    early = PER

    def co_step(t, carry):
        gc.from_below(t)
        gc.from_above(t)

        @pl.when(t < UNITS - 1)
        def _():
            gc.x_arrival(at.z, t)

        gc.beside_far(t - PER)

        @pl.when(jnp.logical_and(t >= steps - early, at.z < last))
        def _():
            gs.in_order(t - (steps - early) - at.z)

        return carry

    lax.fori_loop(0, steps - early, co_step, 0)
    gs.start(False)
    gs.other_last(False)
    lax.fori_loop(steps - early, steps, co_step, 0)

    def co_rest(t, carry):
        gc.beside_far(t)
        return carry

    lax.fori_loop(steps - PER, steps, co_rest, 0)
    gs.beside_own()
    for zo in range(line):
        gc.arrived(zo)
    states.wait_recv()

    ahead = jnp.where(at.z < last, early - at.z, 0)

    def self_beside(t):
        gs.beside_order(t + ahead)
        gs.beside_above(t)

    def self_steps(a, b, lag):
        def step(t, carry):
            gs.in_order(t + ahead)
            gs.from_above(t)
            self_beside(t - lag)
            return carry

        lax.fori_loop(a, b, step, 0)

    def self_rest(a, b):
        lax.fori_loop(a, b, lambda t, carry: (self_beside(t), carry)[1], 0)

    gather_steps = steps
    scatter_ticks = 20

    def run(text, co, sa):
        rows, width = co.rows, co.width

        def view(refs, b):
            d = {name: View(ref, kept_shapes(b)[name]) for name, ref in refs.items()}
            for name, ref in shared.items():
                d[name] = View(ref, shared_shapes(b)[name])
            for k, name in enumerate(("r1", "r2")):
                d[name] = Pooled(pool, (2 * (b is sa) + k) * span, b.rows, b.width)
            d["h"], d["dy"] = [Pooled(pool, k * span, b.rows, b.width) for k in (4, 5)]
            d["small"] = small
            return d

        a = Net(co, wc, vec, view(sc, co))
        b = Net(sa, ws, vec2, view(ss, sa))
        h, hb, dy = b.s["h"], b.s["hb"], b.s["dy"]

        own_in = View(xin, (rows, width))
        if text:
            to_flat(flat, xbox)

            def put(j, value):
                own_in[:, cols(j, 128)] = value.astype(BF16)

            from_flat(flat, rows, width // 128, put)
            x, z = own_in, View(xp, xp.shape)
        else:
            to_flat(flat, xp)
            other = View(xin, (co.other_rows, co.other))

            def put(j, value):
                other[:, cols(j, 128)] = value.astype(BF16)

            from_flat(flat, co.other_rows, co.other // 128, put)
            x, z = View(xbox, xbox.shape), other

        steps_done, beside_done, places = [0], [-PER], [0]

        def tick(k=1):
            a0 = steps_done[0]
            b0 = min(a0 + k, gather_steps)
            if b0 > a0:
                self_steps(a0, b0, a0 - beside_done[0])
                beside_done[0] += b0 - a0
                steps_done[0] = b0

        def need(name):
            later = [sa.place[n][0] for n in ("i_w", "f_w") if sa.place[n][0] > sa.place[name][0]]
            top = -(-min(later + [sa.tiles]) // (4 * gs.rows))
            wanted = min(PER * top, gather_steps)
            tick(min(wanted + 3, gather_steps) - steps_done[0])
            if beside_done[0] < wanted:
                self_rest(beside_done[0], wanted)
                beside_done[0] = wanted
            for zo in range(places[0], top):
                gs.arrived(zo)
            places[0] = max(places[0], top)

        value = a.forward(x, x, z, lambda q: lens[1, q], tick)
        h[...] = value
        hb[...] = value.astype(BF16)
        gc.sent()
        if text:
            to_flat(flat, gbox)

            def put(j, value):
                dy[:, cols(j, 128)] = value

            from_flat(flat, rows, width // 128, put)
        else:
            dy[...] = gbox[...].astype(F32)
        value = b.forward(h, hb, hb, lambda q: lens[0, q], tick, need)
        if text:
            for j in range(width // 128):
                flat[pl.ds(j, rows, stride=width // 128), :] = value[:, j * 128 : (j + 1) * 128]
        else:
            out_box[...] = value.astype(BF16)
        gs.sent()

        def put_h(c, value):
            h[:, c] = value

        def add_h(c, value):
            h[:, c] = h[:, c] + value

        ticks = [0]

        def hooks(scatter, block):
            state = [line]

            def done(name):
                tile = block.place[name][0]
                ready = -(-tile // (4 * scatter.rows))
                while state[0] > ready:
                    state[0] -= 1
                    scatter.ready(state[0])
                    if scatter is rs and state[0] == last:
                        rs.prepare(0)

            return done

        def rs_tick(k=1):
            a0 = ticks[0]
            ticks[0] = a0 + k
            lax.fori_loop(a0, a0 + k, lambda t, carry: (rs.slot(t), carry)[1], 0)

        b.backward(dy, hb, hb, put_h, add_h, hooks(rs, sa), rs_tick)
        if text:
            def put(j, value):
                out_box[:, j * 128 : (j + 1) * 128] = value.astype(BF16)

            from_flat(flat, out_box.shape[0], out_box.shape[1] // 128, put)

        def put_own(c, value):
            dy[:, c] = value

        sent_rows = View(sent, (co.other_rows, co.other))

        def put_sent(c, value):
            sent_rows[:, c] = value.astype(BF16)

        a.backward(h, x, z, put_own, put_sent, hooks(rc, co), rs_tick)
        over(1, sent, ret).start()
        assert ticks[0] <= scatter_ticks, ticks[0]
        if ticks[0] < scatter_ticks:
            rs_tick(scatter_ticks - ticks[0])

    for s, (co, sa) in enumerate(kinds):
        @pl.when(at.s == s)
        def _(s=s, co=co, sa=sa):
            run(s == 0, co, sa)

    rc.prepare(0)
    es.clear()
    shift = rs.items
    steps = shift + rc.slots

    def both(t, carry):
        @pl.when(t < rs.slots)
        def _():
            rs.slot(t, True)

        @pl.when(t == rs.slots)
        def _():
            es.give()

        @pl.when(t == rs.slots + 2)
        def _():
            es.finish(sa_out)

        @pl.when(t == rs.slots + 4)
        def _():
            es.done(sa_out)
            ec.clear()

        @pl.when(t >= shift)
        def _():
            rc.slot(t - shift, True)

        return carry

    assert rs.slots + 4 < shift + rc.final
    lax.fori_loop(scatter_ticks, steps, both, 0)
    ec.give()

    back = over(1, sent, ret)
    back.wait_recv()
    for s, (co, sa) in enumerate(kinds):
        @pl.when(at.s == s)
        def _(s=s, co=co):
            mine = Pooled(pool, 5 * span, co.rows, co.width)
            got = View(ret, (co.rows, co.width))
            if s == 0:
                count = co.width // 128
                for j in range(count):
                    flat[pl.ds(j, co.rows, stride=count), :] = mine[:, cols(j, 128)] + got[:, cols(j, 128)].astype(F32)

                def put(j, value):
                    grad_box[:, j * 128 : (j + 1) * 128] = value

                from_flat(flat, grad_box.shape[0], grad_box.shape[1] // 128, put)
            else:
                grad_box[...] = mine[...] + got[...].astype(F32)

    ec.finish(co_out)
    back.wait_send()
    states.wait_send()
    rs.sent()
    rc.sent()
    ec.done(co_out)


KEPT = ("q", "k", "v", "p", "c", "y1", "a", "gp")
SHARED = ("fill", "m", "hb", "dc")


def kept_shapes(b):
    return {k: v[0] for k, v in scratch_of(b).items()}


def shared_shapes(b):
    rows, width = b.rows, b.width
    return {"fill": (b.rows, b.other_rows), "m": (rows, width), "hb": (rows, width), "dc": (rows, b.inner)}


SHARED_TYPES = {"fill": F32}


def most(shapes):
    return tuple(max(k) for k in zip(*shapes))


def pool_span(plans):
    return max(b.rows * b.width // 128 for p in plans for b in p.blocks)


def layer_call(plans, line, lens, xbox, gbox, co_flat, sa_flat, cid):
    vm = pl.BlockSpec(memory_space=pltpu.VMEM)
    any_ = pl.BlockSpec(memory_space=pl.ANY)
    rows_c, rows_s = [p.rows for p in plans]
    V = pltpu.VMEM
    cos, sas = [p.blocks for p in plans]
    wide = most([(b.rows, b.width) for b in cos] + [(b.other_rows, b.other) for b in cos])
    n = max(rows_c, rows_s) // UNITS
    edge = sum(p.before + p.after for p in plans)
    assert max(p.window for p in plans) + edge <= 5 * pool_span(plans)
    scr = [V((plans[0].tiles, 16, 128), BF16), V((plans[1].tiles, 16, 128), BF16), V((16, 3072), F32), V((16, 3072), F32), V((32, 128), F32),
           V((7 * pool_span(plans), 128), F32), V((edge, 128), F32), V(xbox.shape, BF16), V(wide, BF16), V(wide, BF16),
           V((12, rows_c // UNITS, 16, 128), BF16), V((12, rows_s // UNITS, 16, 128), BF16), V((n, 16, 128), F32)]
    for bs in (cos, sas):
        for name in sorted(KEPT):
            scr.append(V(most([kept_shapes(b)[name] for b in bs]), scratch_of(bs[0])[name][1]))
    for name in sorted(SHARED):
        shape = most([shared_shapes(b)[name] for b in cos + sas] + ([wide] if name == "dc" else []))
        scr.append(V(shape, SHARED_TYPES.get(name, BF16)))
    dma = pltpu.SemaphoreType.DMA
    scr += gather_sems(line) + gather_sems(line) + scatter_sems(line) + scatter_sems(line) + edge_sems() + edge_sems() + [dma((2,)), dma((2,))]
    struct = jax.ShapeDtypeStruct
    outs = [struct(xbox.shape, BF16), struct(xbox.shape, F32), struct(co_flat.shape, F32), struct(sa_flat.shape, F32)]
    outs += landing(line, rows_c) + landing(line, rows_s)
    return pl.pallas_call(
        functools.partial(layer_kernel, plans, line),
        out_shape=outs,
        in_specs=[pl.BlockSpec(memory_space=pltpu.SMEM), vm, vm, any_, any_],
        out_specs=[vm, vm] + [any_] * 8,
        scratch_shapes=scr,
        compiler_params=pltpu.CompilerParams(collective_id=cid, has_side_effects=True, vmem_limit_bytes=64 * 2**20 - 2**16),
        name="layer",
    )(lens, xbox, gbox, co_flat, sa_flat)[:4]


DT, HT, FT = 768, 12, 3072
DI, HI, FI = 1024, 8, 1024
DC, HC = 1024, 8
LT, LI = 128, 96
LINE_MAX = 8


def blocks_of(text, seqs):
    if text:
        return (Block(DT, DI, DC, FT, HC, LT, LI, seqs), Block(DT, DT, DT, FT, HT, LT, LT, seqs))
    return (Block(DI, DT, DC, FI, HC, LI, LT, seqs), Block(DI, DI, DI, FI, HI, LI, LI, seqs))


class Plan:
    def __init__(self, blocks, devices, flat_total):
        self.blocks = blocks
        self.shard = flat_total // 128 // devices
        tiles = max(b.tiles for b in blocks)
        self.rows = -(-tiles // (devices * UNITS)) * UNITS
        self.tiles = self.rows * devices
        tables = [self.table(b).reshape(self.tiles, 16) for b in blocks]
        before = after = 0
        for table in tables:
            most = table.max(axis=1)
            least = np.where(table >= 0, table, flat_total).min(axis=1)
            for d in range(devices):
                lo, hi, start, end = self.rows * d, self.rows * (d + 1), self.shard * d, self.shard * (d + 1)
                held = np.nonzero(most[lo:hi] >= 0)[0] + lo
                if held.size:
                    before = max(before, start - least[held].min())
                    after = max(after, most[held].max() + 1 - end)
        self.before, self.after = [max(-(-int(k) // 16) * 16, 16) for k in (before, after)]
        self.window = -(-(self.before + self.shard + self.after) // 8) * 8
        self.near = max(self.before, self.after) <= self.shard

    def table(self, b):
        index = np.full((self.tiles * 16,), -1, np.int32)
        for first, flat, k, rows, nb in b.parts:
            if k:
                r, j = np.arange(k)[:, None], np.arange(nb)[None]
                at = first * 16 + ((r // 16) * nb + j) * 16 + r % 16
                index[at.reshape(-1)] = (flat + r * nb + j).reshape(-1)
            else:
                index[first * 16 : first * 16 + rows] = flat + np.arange(rows)
        return index


def each_tile(b, lo, hi, start, act):
    for first, flat, k, rows, nb in b.parts:
        if k:
            count = rows // 16
            a = jnp.clip(lo - first, 0, count)
            z = jnp.clip(hi - first, 0, count)

            def body(t, carry, first=first, flat=flat, nb=nb):
                i = t // nb
                act(first + t, flat + i * 16 * nb + (t - i * nb) - start, nb, 16)
                return carry

            lax.fori_loop(a, z, body, 0)
        else:
            for t in range((rows + 15) // 16):
                @pl.when(jnp.logical_and(first + t >= lo, first + t < hi))
                def _(t=t, first=first, flat=flat, rows=rows):
                    act(first + t, flat + 16 * t - start, 1, min(16, rows - 16 * t))


def gathered(plan, text, flat):
    whole = lax.all_gather(flat.astype(BF16), "dp", axis=0, tiled=True).reshape(-1, 128)
    index = jnp.where(text, *[jnp.asarray(plan.table(b)) for b in plan.blocks])
    rows = jnp.where((index >= 0)[:, None], whole[jnp.maximum(index, 0)], jnp.zeros((), BF16))
    return rows.reshape(plan.tiles, 16, 128)


def scattered(plan, text, tiles, flat_rows):
    tables = []
    for b in plan.blocks:
        table = plan.table(b)
        back = np.full((flat_rows,), -1, np.int32)
        held = np.nonzero(table >= 0)[0]
        back[table[held]] = held
        tables.append(jnp.asarray(back))
    index = jnp.where(text, *tables)
    rows = jnp.where((index >= 0)[:, None], tiles.reshape(-1, 128)[jnp.maximum(index, 0)], jnp.zeros((), BF16))
    return lax.psum_scatter(rows.astype(F32), "dp", scatter_dimension=0, tiled=True).reshape(-1)


def layer_alone(text, counts, own, partner, grad, wco, wsa):
    seqs = own.shape[0]
    co, sa = blocks_of(text, seqs)
    box = own.shape
    lens = counts if text else counts[::-1]
    out, own_grad, sent, gco, gsa = compute(
        co, sa, lens, own.reshape(co.rows, co.width), partner.reshape(co.other_rows, co.other),
        grad.reshape(co.rows, co.width), wco, wsa)
    return out.reshape(box), own_grad.reshape(box), sent.reshape(box), gco, gsa


def body(devices, states, out_grad, co_params, self_params, text_lengths, region_counts):
    own = states[0]
    seqs = own.shape[0]
    text = lax.axis_index("stream") == 0
    flats = (co_params[0], self_params[0])
    streams = [blocks_of(t, seqs) for t in (True, False)]
    plans = [Plan([k[i] for k in streams], devices, f.shape[0] * devices) for i, f in enumerate(flats)]
    line = devices // 4
    counts = jnp.stack([text_lengths, region_counts])
    if devices % 4 == 0 and line <= LINE_MAX and all(p.near for p in plans):
        lens = jnp.where(text, counts, counts[::-1])
        box = (own.shape[0] * own.shape[1], own.shape[2])
        flats = [f.reshape(p.shard, 1, 128) for p, f in zip(plans, flats)]
        out, grad, co_grad, sa_grad = layer_call(plans, line, lens, own.reshape(box), out_grad[0].reshape(box), *flats, 1)
        return (out.reshape(states.shape), grad.reshape(states.shape), co_grad.reshape(co_params.shape), sa_grad.reshape(self_params.shape))
    swap = [(0, 1), (1, 0)]
    partner = lax.ppermute(own, "stream", swap)
    wco, wsa = [gathered(p, text, f) for p, f in zip(plans, flats)]
    out, own_grad, sent, gco, gsa = lax.cond(
        text, functools.partial(layer_alone, True), functools.partial(layer_alone, False),
        counts, own, partner, out_grad[0], wco, wsa)
    returned = lax.ppermute(sent, "stream", swap)
    flats = [scattered(p, text, g, p.shard * devices) for p, g in zip(plans, (gco, gsa))]
    return (out[None], (own_grad + returned.astype(F32))[None], flats[0][None], flats[1][None])


def solution(mesh):
    states = P("stream", "dp", None, None)
    flat = P("stream", "dp")
    return jax.shard_map(
        functools.partial(body, mesh.shape["dp"]), mesh=mesh, in_specs=(states, states, flat, flat, P("dp"), P("dp")),
        out_specs=(states, states, flat, flat), check_vma=False)
```

profile of v0, /device:TPU:9, one launch (start us, length us, event | category | flops | bytes accessed | tf_op | source)
XLA Modules:
  0.0 422.3 jit_solution(12320278127587720309)
XLA Ops:
  0.6 0.7 pad_add_fusion
  1.3 1.2 broadcast_select_fusion.lens
  2.6 412.8 %layer.1 = (bf16[192,1024]{1,0:T(8,128)(2,1)}, f32[192,1024]{1,0:T(8,128)}, f32[4101,1,128]{2,1,0:T(1,128)}, f32[3461,1,128]{2,1,0:T(1,128)}, bf16[8,258,16,128]...) custom-call(s32[2,2]{1,0:T(2,128)} %broadcast_select_fusion.lens, ...), custom_call_target="tpu_custom_call" | custom-call | tf_op jit(solution)/shard_map/layer/pallas_call | solution.py:1407
  415.4 0.0 copy-start
  415.4 0.0 copy-start.1
  415.5 1.9 copy.14
  417.4 2.1 copy.15
  419.5 0.0 copy-done
  419.5 1.3 copy.16
  420.8 0.0 copy-done.1
  420.8 1.2 copy.17
  (1 shorter events, 0.0 us)
Async XLA Ops:
  415.4 4.0 copy-start
  415.4 5.3 %copy-start.1 = (f32[3461,1,128]{2,1,0:T(1,128)S(1)}, f32[3461,1,128]{2,1,0:T(1,128)}, u32[]{:S(2)}) copy-start(f32[3461,1,128]{2,1,0:T(1,128)} %get-tuple-element.11) | copy-start | bytes 5316100
where the time goes:
time: 428 us; the launch traced here: 422 us
  Pallas kernels  413 us (96%)
  local copies, waits for them, and re-layouts  6.57 us (2%)
    pallas_call x1, Pallas kernels, layer_call(): pl.pallas_call(functools.partial(layer_kernel, plans, line), out_shape=ou...  413 us

commit v1 on v0

--- a/solution.py
+++ b/solution.py
@@ -280,7 +280,7 @@
             c[:, cols(g, 128)] = total.astype(BF16)
             return carry
 
-        lax.fori_loop(0, b.inner // 128, body, 0, unroll=True)
+        lax.fori_loop(0, b.inner // 128, body, 0, unroll=2)
 
     def attend_back(self, q, k, v, p, dc):
         b = self.b
@@ -303,7 +303,7 @@
             v[:, cols(g, 128)] = sums[2].astype(BF16)
             return carry
 
-        lax.fori_loop(0, b.inner // 128, body, 0, unroll=True)
+        lax.fori_loop(0, b.inner // 128, body, 0, unroll=2)
 
     def forward(self, x, u, z, counts, tick=lambda k=1: None, need=lambda name: None):
         s, b = self.s, self.b
@@ -371,14 +371,13 @@
         self.store_vectors(GROUPS[4], small)
         self.tn(s["a"], s["m"], "f_w")
         done("f_w")
-        tick()
         self.put_sum("i_b", s["gp"])
 
         def mid(c, value):
             dy[:, c] = dy[:, c] + value
 
         self.nt(s["gp"], "i_w", mid)
-        tick()
+        tick(4)
         self.store_vectors(GROUPS[3], small)
         self.tn(s["y1"], s["gp"], "i_w")
         done("i_w")
@@ -395,7 +394,7 @@
         self.store_vectors(GROUPS[2], small)
         self.tn(s["c"], s["m"], "o_w")
         done("o_w")
-        tick(2)
+        tick(3)
         self.attend_back(s["q"], s["k"], s["v"], s["p"], s["dc"])
 
         tick(2)
@@ -422,7 +421,7 @@
         self.tn(z, s["k"], "k_w")
         self.tn(z, s["v"], "v_w")
         done("q_w")
-        tick()
+        tick(2)
 
 
 def scratch_of(b):
@@ -508,8 +507,8 @@
 
 
 PER = UNITS + 1
-BEHIND = 4
-LEAD = 3
+SLOTS_TEXT, SLOTS_IMAGE, SLOTS_CO = (2, 4, 3, 2, 1, 1), (2, 0, 4, 2, 1, 4), (1, 1, 0, 1, 0, 1)
+BEHIND = 2
 
 
 class Where:
@@ -557,8 +556,11 @@
         self.n = self.rows // UNITS
         self.up_s, self.dn_s, self.z_r, self.x_s, self.x_r, self.c_s, self.c_r, self.o_s = sems
 
+    def lies(self, u):
+        return jnp.where(u == 0, 1, jnp.where(u < 4, u + 2, jnp.where(u == 4, 0, 2))) * self.n
+
     def spot(self, zo, xb, cc, u):
-        return self.w.at[pl.ds(((zo * 2 + xb) * 2 + cc) * self.rows + u * self.n, self.n)]
+        return self.w.at[pl.ds(((zo * 2 + xb) * 2 + cc) * self.rows + self.lies(u), self.n)]
 
     def block_of(self, v):
         x = self.at.x
@@ -590,19 +592,29 @@
     def first(self):
         self.x_copy(self.at.z, UNITS - 1, first=True).start()
 
-    def start(self, up):
-        at = self.at
-        z, x = at.z, at.x
+    def start_unit(self, u):
+        at = self.at
+
+        @pl.when(u == UNITS - 1)
+        def _():
+            self.first()
+
+        @pl.when(u != UNITS - 1)
+        def _():
+            self.x_copy(at.z, u).start()
+
+        self.send_z(at.z, u, True)
+        self.send_z(at.z, u, False)
+        self.c_copy(at.z, at.x, u).start()
+
+    def start(self):
+        at = self.at
         for u in range(UNITS - 1):
-            self.x_copy(z, u).start()
-            self.send_z(z, u, False)
-            if up:
-                self.send_z(z, u, True)
-        self.send_z(z, UNITS - 1, False)
-        if up:
-            self.send_z(z, UNITS - 1, True)
+            self.x_copy(at.z, u).start()
+            self.send_z(at.z, u, False)
+        self.send_z(at.z, UNITS - 1, False)
         for u in range(UNITS):
-            self.c_copy(z, x, u).start()
+            self.c_copy(at.z, at.x, u).start()
 
     def other_last(self, up):
         at = self.at
@@ -722,17 +734,21 @@
 
 
 class Scatter:
-    def __init__(self, at, g, rows, cr, xr, zr, keep, stage, wide_stage, behind, sems):
+    def __init__(self, at, g, rows, cr, xr, zr, keep, stage, wide_stage, behind, lead, sems):
         self.at, self.g, self.rows, self.n = at, g, rows, rows // UNITS
         self.cr, self.xr, self.zr, self.keep, self.stage, self.wide = cr, xr, zr, keep, stage, wide_stage
         self.c_s, self.c_r, self.x_s, self.x_r, self.z_s, self.z_r, self.l_s, self.b_s = sems
+        self.lead = lead
         self.behind = behind
         self.items = at.last * PER
-        self.final = self.items + LEAD + at.last + behind
+        self.final = self.items + lead + at.last + behind
         self.slots = self.final + PER
 
+    def lies(self, u):
+        return (u + UNITS // 2) % UNITS * self.n if isinstance(u, int) else lax.rem(u + UNITS // 2, UNITS) * self.n
+
     def mine(self, zo, xb, u):
-        return pl.ds(((zo * 2 + xb) * 2 + self.at.c) * self.rows + u * self.n, self.n)
+        return pl.ds(((zo * 2 + xb) * 2 + self.at.c) * self.rows + self.lies(u), self.n)
 
     def block_of(self, v):
         x = self.at.x
@@ -770,7 +786,7 @@
         return pltpu.make_async_copy(src, self.stage.at[slot, pl.ds(0, self.n)], self.l_s.at[slot])
 
     def core_part(self, zo, xb, u):
-        return self.cr.at[zo * 2 + xb, pl.ds(u * self.n, self.n)]
+        return self.cr.at[zo * 2 + xb, pl.ds(self.lies(u), self.n)]
 
     def way(self, t, up):
         at = self.at
@@ -785,12 +801,12 @@
         for up, slot in ((True, 0), (False, 11)):
             to, v, here = self.way(t, up)
             found.append((to, v - 1, jnp.logical_and(here, jnp.logical_and(v >= 1, v < UNITS)), slot))
-        u = t - self.items - self.behind - 1
-        found.append((at.z, u, jnp.logical_and(u >= 0, u < UNITS - 1), 0))
+        u = t - self.items - 1
+        found.append((at.z, u, jnp.logical_and(u >= 0, u < UNITS - 1), 12))
         return found
 
     def parts(self, t, finals):
-        found = [self.way(t - LEAD, up) + (up, slot) for up, slot in ((True, 1), (False, 4))]
+        found = [self.way(t - self.lead, up) + (up, slot) for up, slot in ((True, 1), (False, 4))]
         own = t - self.final
         return found + [(self.at.z, own, jnp.logical_and(own >= 0, own < PER), None, 7)] * finals
 
@@ -871,7 +887,7 @@
 
                     @pl.when(v >= 1)
                     def _():
-                        self.keep(u)
+                        self.keep(self.lies(u))
                 else:
                     @pl.when(at.z != (0 if up else at.last))
                     def _():
@@ -914,7 +930,7 @@
 
 def scatter_sems(line):
     dma = pltpu.SemaphoreType.DMA
-    return [dma((line,)), dma((line * 2,)), dma((line,)), dma((line * UNITS,)), dma((line,)), dma(((line + 1) * PER,)), dma((12,)), dma]
+    return [dma((line,)), dma((line * 2,)), dma((line,)), dma((line * UNITS,)), dma((line,)), dma(((line + 1) * PER,)), dma((13,)), dma]
 
 
 def landing(line, rows):
@@ -960,11 +976,12 @@
     def inner(self, own):
         return pltpu.make_async_copy(own.at[:, 0], self.window.at[pl.ds(self.plan.before, self.plan.shard)], self.l_s)
 
-    def tiles(self, kinds, own, w):
+    def clear_tiles(self, w):
+        w[pl.ds(self.plan.rows * self.d, self.plan.rows)] = jnp.zeros((self.plan.rows, 16, 128), w.dtype)
+
+    def enter(self, own):
         plan = self.plan
         up, down = self.outer(own)
-        lo = plan.rows * self.d
-        w[pl.ds(lo, plan.rows)] = jnp.zeros((plan.rows, 16, 128), w.dtype)
 
         def above():
             down.wait_recv()
@@ -975,7 +992,9 @@
             self.window[: plan.before, :] = self.first[: plan.before, :]
 
         self.both(above, below)
-        self.inner(own).wait()
+
+    def tiles(self, kinds, w, first, count):
+        lo = self.plan.rows * self.d + first
 
         def act(tile, row, stride, rows):
             value = self.window[pl.ds(row, rows, stride=stride), :]
@@ -983,7 +1002,10 @@
                 value = jnp.concatenate([value, jnp.zeros((16 - rows, 128), value.dtype)], axis=0)
             w[tile] = value.astype(w.dtype)
 
-        self.by_stream(kinds, lo, lo + plan.rows, act)
+        self.by_stream(kinds, lo, lo + count, act)
+
+    def entered(self, own):
+        up, down = self.outer(own)
         self.both(up.wait_send, down.wait_send)
 
     def by_stream(self, kinds, lo, hi, act):
@@ -997,8 +1019,8 @@
         self.window[...] = jnp.zeros(self.window.shape, F32)
 
     def take(self, kinds, acc, n):
-        def keep(u):
-            lo = self.plan.rows * self.d + u * n
+        def keep(first):
+            lo = self.plan.rows * self.d + first
 
             def act(tile, row, stride, rows):
                 self.window[pl.ds(row, rows, stride=stride), :] = acc[tile - lo][:rows]
@@ -1060,7 +1082,7 @@
         put(j, flat[pl.ds(j, rows, stride=count), :])
 
 
-def layer_kernel(plans, line, lens, xbox, gbox, co_flat, sa_flat, *refs):
+def layer_kernel(plans, line, texts, regions, xbox, gbox, co_flat, sa_flat, *refs):
     kinds = list(zip(plans[0].blocks, plans[1].blocks))
     outs, refs = refs[:10], refs[10:]
     out_box, grad_box, co_out, sa_out = outs[:4]
@@ -1089,8 +1111,8 @@
                            land.at[pl.ds(k * sizes[0], sizes[k])], sems))
     ec, es = edges
     own_kinds = [[k[i] for k in kinds] for i in range(2)]
-    rc = Scatter(at, wc, plans[0].rows, *outs[4:7], ec.take(own_kinds[0], acc, gc.n), stage_c, acc, 0, rs_c)
-    rs = Scatter(at, ws, plans[1].rows, *outs[7:10], es.take(own_kinds[1], acc, gs.n), stage_s, acc, BEHIND, rs_s)
+    rc = Scatter(at, wc, plans[0].rows, *outs[4:7], ec.take(own_kinds[0], acc, gc.n), stage_c, acc, 0, 5, rs_c)
+    rs = Scatter(at, ws, plans[1].rows, *outs[7:10], es.take(own_kinds[1], acc, gs.n), stage_s, acc, BEHIND, 3, rs_s)
 
     def over(k, src, dst):
         return at.copy(src, dst, y_s.at[k], y_r.at[k], at.z, at.x, at.c, 1 - at.s)
@@ -1099,13 +1121,29 @@
     at.greet()
     ec.send(co_flat)
     es.send(sa_flat)
-    ec.tiles(own_kinds[0], co_flat, wc)
-    gc.first()
-    gc.start(True)
+    ec.clear_tiles(wc)
+    ec.inner(co_flat).wait()
+
+    def begin(k, carry):
+        @pl.when(k == 2)
+        def _():
+            ec.enter(co_flat)
+
+        u = lax.rem(k + UNITS - 1, UNITS)
+        ec.tiles(own_kinds[0], wc, gc.lies(u), gc.n)
+        gc.start_unit(u)
+        return carry
+
+    lax.fori_loop(0, UNITS, begin, 0)
     es.inner(sa_flat).start()
     states = over(0, xbox, xp)
     states.start()
-    es.tiles(own_kinds[1], sa_flat, ws)
+    ec.entered(co_flat)
+    es.clear_tiles(ws)
+    es.inner(sa_flat).wait()
+    es.enter(sa_flat)
+    es.tiles(own_kinds[1], ws, 0, plans[1].rows)
+    es.entered(sa_flat)
     gs.first()
     gc.other_last(True)
 
@@ -1129,7 +1167,7 @@
         return carry
 
     lax.fori_loop(0, steps - early, co_step, 0)
-    gs.start(False)
+    gs.start()
     gs.other_last(False)
     lax.fori_loop(steps - early, steps, co_step, 0)
 
@@ -1162,7 +1200,7 @@
         lax.fori_loop(a, b, lambda t, carry: (self_beside(t), carry)[1], 0)
 
     gather_steps = steps
-    scatter_ticks = 20
+    scatter_ticks = sum(SLOTS_TEXT) + sum(SLOTS_CO)
 
     def run(text, co, sa):
         rows, width = co.rows, co.width
@@ -1222,7 +1260,8 @@
                 gs.arrived(zo)
             places[0] = max(places[0], top)
 
-        value = a.forward(x, x, z, lambda q: lens[1, q], tick)
+        own_counts, other_counts = (texts, regions) if text else (regions, texts)
+        value = a.forward(x, x, z, lambda q: other_counts[q], tick)
         h[...] = value
         hb[...] = value.astype(BF16)
         gc.sent()
@@ -1235,7 +1274,7 @@
             from_flat(flat, rows, width // 128, put)
         else:
             dy[...] = gbox[...].astype(F32)
-        value = b.forward(h, hb, hb, lambda q: lens[0, q], tick, need)
+        value = b.forward(h, hb, hb, lambda q: own_counts[q], tick, need)
         if text:
             for j in range(width // 128):
                 flat[pl.ds(j, rows, stride=width // 128), :] = value[:, j * 128 : (j + 1) * 128]
@@ -1265,12 +1304,17 @@
 
             return done
 
-        def rs_tick(k=1):
+        def slots(k):
             a0 = ticks[0]
             ticks[0] = a0 + k
-            lax.fori_loop(a0, a0 + k, lambda t, carry: (rs.slot(t), carry)[1], 0)
-
-        b.backward(dy, hb, hb, put_h, add_h, hooks(rs, sa), rs_tick)
+            if k:
+                lax.fori_loop(a0, a0 + k, lambda t, carry: (rs.slot(t), carry)[1], 0)
+
+        def rs_tick(counts):
+            left = list(counts)
+            return lambda k=1: slots(left.pop(0))
+
+        b.backward(dy, hb, hb, put_h, add_h, hooks(rs, sa), rs_tick(SLOTS_TEXT if text else SLOTS_IMAGE))
         if text:
             def put(j, value):
                 out_box[:, j * 128 : (j + 1) * 128] = value.astype(BF16)
@@ -1285,17 +1329,36 @@
         def put_sent(c, value):
             sent_rows[:, c] = value.astype(BF16)
 
-        a.backward(h, x, z, put_own, put_sent, hooks(rc, co), rs_tick)
+        a.backward(h, x, z, put_own, put_sent, hooks(rc, co), rs_tick(SLOTS_CO))
         over(1, sent, ret).start()
-        assert ticks[0] <= scatter_ticks, ticks[0]
-        if ticks[0] < scatter_ticks:
-            rs_tick(scatter_ticks - ticks[0])
+        assert ticks[0] == scatter_ticks
 
     for s, (co, sa) in enumerate(kinds):
         @pl.when(at.s == s)
         def _(s=s, co=co, sa=sa):
             run(s == 0, co, sa)
 
+    back = over(1, sent, ret)
+
+    def grads_of_states():
+        back.wait_recv()
+        for s, (co, sa) in enumerate(kinds):
+            @pl.when(at.s == s)
+            def _(s=s, co=co):
+                mine = Pooled(pool, 5 * span, co.rows, co.width)
+                got = View(ret, (co.rows, co.width))
+                if s == 0:
+                    count = co.width // 128
+                    for j in range(count):
+                        flat[pl.ds(j, co.rows, stride=count), :] = mine[:, cols(j, 128)] + got[:, cols(j, 128)].astype(F32)
+
+                    def put(j, value):
+                        grad_box[:, j * 128 : (j + 1) * 128] = value
+
+                    from_flat(flat, grad_box.shape[0], grad_box.shape[1] // 128, put)
+                else:
+                    grad_box[...] = mine[...] + got[...].astype(F32)
+
     rc.prepare(0)
     es.clear()
     shift = rs.items
@@ -1318,40 +1381,27 @@
         def _():
             es.done(sa_out)
             ec.clear()
+            rs.sent()
+
+        @pl.when(t == shift + rc.final - 1)
+        def _():
+            grads_of_states()
 
         @pl.when(t >= shift)
         def _():
             rc.slot(t - shift, True)
+
+        @pl.when(t == shift + rc.final + 4)
+        def _():
+            ec.give()
 
         return carry
 
     assert rs.slots + 4 < shift + rc.final
     lax.fori_loop(scatter_ticks, steps, both, 0)
-    ec.give()
-
-    back = over(1, sent, ret)
-    back.wait_recv()
-    for s, (co, sa) in enumerate(kinds):
-        @pl.when(at.s == s)
-        def _(s=s, co=co):
-            mine = Pooled(pool, 5 * span, co.rows, co.width)
-            got = View(ret, (co.rows, co.width))
-            if s == 0:
-                count = co.width // 128
-                for j in range(count):
-                    flat[pl.ds(j, co.rows, stride=count), :] = mine[:, cols(j, 128)] + got[:, cols(j, 128)].astype(F32)
-
-                def put(j, value):
-                    grad_box[:, j * 128 : (j + 1) * 128] = value
-
-                from_flat(flat, grad_box.shape[0], grad_box.shape[1] // 128, put)
-            else:
-                grad_box[...] = mine[...] + got[...].astype(F32)
-
     ec.finish(co_out)
     back.wait_send()
     states.wait_send()
-    rs.sent()
     rc.sent()
     ec.done(co_out)
 
@@ -1380,7 +1430,7 @@
     return max(b.rows * b.width // 128 for p in plans for b in p.blocks)
 
 
-def layer_call(plans, line, lens, xbox, gbox, co_flat, sa_flat, cid):
+def layer_call(plans, line, texts, regions, xbox, gbox, co_flat, sa_flat, cid):
     vm = pl.BlockSpec(memory_space=pltpu.VMEM)
     any_ = pl.BlockSpec(memory_space=pl.ANY)
     rows_c, rows_s = [p.rows for p in plans]
@@ -1392,7 +1442,7 @@
     assert max(p.window for p in plans) + edge <= 5 * pool_span(plans)
     scr = [V((plans[0].tiles, 16, 128), BF16), V((plans[1].tiles, 16, 128), BF16), V((16, 3072), F32), V((16, 3072), F32), V((32, 128), F32),
            V((7 * pool_span(plans), 128), F32), V((edge, 128), F32), V(xbox.shape, BF16), V(wide, BF16), V(wide, BF16),
-           V((12, rows_c // UNITS, 16, 128), BF16), V((12, rows_s // UNITS, 16, 128), BF16), V((n, 16, 128), F32)]
+           V((13, rows_c // UNITS, 16, 128), BF16), V((13, rows_s // UNITS, 16, 128), BF16), V((n, 16, 128), F32)]
     for bs in (cos, sas):
         for name in sorted(KEPT):
             scr.append(V(most([kept_shapes(b)[name] for b in bs]), scratch_of(bs[0])[name][1]))
@@ -1407,12 +1457,12 @@
     return pl.pallas_call(
         functools.partial(layer_kernel, plans, line),
         out_shape=outs,
-        in_specs=[pl.BlockSpec(memory_space=pltpu.SMEM), vm, vm, any_, any_],
+        in_specs=[pl.BlockSpec(memory_space=pltpu.SMEM)] * 2 + [vm, vm, any_, any_],
         out_specs=[vm, vm] + [any_] * 8,
         scratch_shapes=scr,
         compiler_params=pltpu.CompilerParams(collective_id=cid, has_side_effects=True, vmem_limit_bytes=64 * 2**20 - 2**16),
         name="layer",
-    )(lens, xbox, gbox, co_flat, sa_flat)[:4]
+    )(texts, regions, xbox, gbox, co_flat, sa_flat)[:4]
 
 
 DT, HT, FT = 768, 12, 3072
@@ -1437,6 +1487,7 @@
         self.tiles = self.rows * devices
         tables = [self.table(b).reshape(self.tiles, 16) for b in blocks]
         before = after = 0
+        inner = True
         for table in tables:
             most = table.max(axis=1)
             least = np.where(table >= 0, table, flat_total).min(axis=1)
@@ -1446,9 +1497,12 @@
                 if held.size:
                     before = max(before, start - least[held].min())
                     after = max(after, most[held].max() + 1 - end)
+                    unit = (held - lo) * UNITS // self.rows
+                    outer = (least[held] < start) & (unit > 0) | (most[held] >= end) & (unit < UNITS // 2)
+                    inner = inner and not outer.any()
         self.before, self.after = [max(-(-int(k) // 16) * 16, 16) for k in (before, after)]
         self.window = -(-(self.before + self.shard + self.after) // 8) * 8
-        self.near = max(self.before, self.after) <= self.shard
+        self.near = max(self.before, self.after) <= self.shard and inner
 
     def table(self, b):
         index = np.full((self.tiles * 16,), -1, np.int32)
@@ -1521,16 +1575,15 @@
     streams = [blocks_of(t, seqs) for t in (True, False)]
     plans = [Plan([k[i] for k in streams], devices, f.shape[0] * devices) for i, f in enumerate(flats)]
     line = devices // 4
-    counts = jnp.stack([text_lengths, region_counts])
     if devices % 4 == 0 and line <= LINE_MAX and all(p.near for p in plans):
-        lens = jnp.where(text, counts, counts[::-1])
         box = (own.shape[0] * own.shape[1], own.shape[2])
         flats = [f.reshape(p.shard, 1, 128) for p, f in zip(plans, flats)]
-        out, grad, co_grad, sa_grad = layer_call(plans, line, lens, own.reshape(box), out_grad[0].reshape(box), *flats, 1)
+        out, grad, co_grad, sa_grad = layer_call(plans, line, text_lengths, region_counts, own.reshape(box), out_grad[0].reshape(box), *flats, 1)
         return (out.reshape(states.shape), grad.reshape(states.shape), co_grad.reshape(co_params.shape), sa_grad.reshape(self_params.shape))
     swap = [(0, 1), (1, 0)]
     partner = lax.ppermute(own, "stream", swap)
     wco, wsa = [gathered(p, text, f) for p, f in zip(plans, flats)]
+    counts = jnp.stack([text_lengths, region_counts])
     out, own_grad, sent, gco, gsa = lax.cond(
         text, functools.partial(layer_alone, True), functools.partial(layer_alone, False),
         counts, own, partner, out_grad[0], wco, wsa)

time: 428 us -> 418 us (0.977)
  Pallas kernels: 413 us -> 405 us
    pallas_call x1, Pallas kernels: 413 us -> 405 us  [layer_call(): pl.pallas_call(functools.partial(layer_kernel, plans, line), out_shape=ou...]
where the time goes in v1:
time: 418 us; the launch traced here: 412 us
  Pallas kernels  405 us (97%)
  local copies, waits for them, and re-layouts  6.54 us (2%)
    pallas_call x1, Pallas kernels, layer_call(): pl.pallas_call(functools.partial(layer_kernel, plans, line), out_shape=ou...  405 us

profile of v1, /device:TPU:9, one launch (start us, length us, event | category | flops | bytes accessed | tf_op | source)
XLA Modules:
  0.0 412.0 jit_solution(9975183634946951476)
XLA Ops:
  0.6 404.6 %layer.1 = (bf16[192,1024]{1,0:T(8,128)(2,1)}, f32[192,1024]{1,0:T(8,128)}, f32[4101,1,128]{2,1,0:T(1,128)}, f32[3461,1,128]{2,1,0:T(1,128)}, bf16[8,258,16,128]...) custom-call(s32[2]{0:T(128)} %texts.1, s32[2]{0:T(128)} %regions.1, ...), custom_call_target="tpu_custom_call" | custom-call | tf_op jit(solution)/shard_map/layer/pallas_call | solution.py:1457
  405.2 0.0 copy-start
  405.2 0.0 copy-start.1
  405.2 1.9 copy.14
  407.1 2.1 copy.15
  409.2 0.0 copy-done
  409.2 1.3 copy.16
  410.5 0.0 copy-done.1
  410.5 1.2 copy.17
Async XLA Ops:
  405.2 4.0 copy-start
  405.2 5.3 %copy-start.1 = (f32[3461,1,128]{2,1,0:T(1,128)S(1)}, f32[3461,1,128]{2,1,0:T(1,128)}, u32[]{:S(2)}) copy-start(f32[3461,1,128]{2,1,0:T(1,128)} %get-tuple-element.11) | copy-start | bytes 5316100

commit v2 on v1

--- a/solution.py
+++ b/solution.py
@@ -508,6 +508,7 @@
 
 PER = UNITS + 1
 SLOTS_TEXT, SLOTS_IMAGE, SLOTS_CO = (2, 4, 3, 2, 1, 1), (2, 0, 4, 2, 1, 4), (1, 1, 0, 1, 0, 1)
+HOP = 3
 BEHIND = 2
 
 
@@ -734,14 +735,15 @@
 
 
 class Scatter:
-    def __init__(self, at, g, rows, cr, xr, zr, keep, stage, wide_stage, behind, lead, sems):
+    def __init__(self, at, g, rows, cr, xr, zr, keep, stage, wide_stage, behind, lead, hop, sems):
         self.at, self.g, self.rows, self.n = at, g, rows, rows // UNITS
         self.cr, self.xr, self.zr, self.keep, self.stage, self.wide = cr, xr, zr, keep, stage, wide_stage
         self.c_s, self.c_r, self.x_s, self.x_r, self.z_s, self.z_r, self.l_s, self.b_s = sems
+        self.hop = hop
         self.lead = lead
         self.behind = behind
         self.items = at.last * PER
-        self.final = self.items + lead + at.last + behind
+        self.final = self.items + lead + at.last * hop + behind
         self.slots = self.final + PER
 
     def lies(self, u):
@@ -790,7 +792,7 @@
 
     def way(self, t, up):
         at = self.at
-        i = t - (at.z if up else at.last - at.z + self.behind)
+        i = t - (at.z * self.hop if up else (at.last - at.z) * self.hop + self.behind)
         to = (at.last if up else at.last - 1) - i // PER
         here = jnp.logical_and(jnp.logical_and(i >= 0, i < self.items), to > at.z if up else to < at.z)
         return to, lax.rem(i, PER), here
@@ -1111,8 +1113,8 @@
                            land.at[pl.ds(k * sizes[0], sizes[k])], sems))
     ec, es = edges
     own_kinds = [[k[i] for k in kinds] for i in range(2)]
-    rc = Scatter(at, wc, plans[0].rows, *outs[4:7], ec.take(own_kinds[0], acc, gc.n), stage_c, acc, 0, 5, rs_c)
-    rs = Scatter(at, ws, plans[1].rows, *outs[7:10], es.take(own_kinds[1], acc, gs.n), stage_s, acc, BEHIND, 3, rs_s)
+    rc = Scatter(at, wc, plans[0].rows, *outs[4:7], ec.take(own_kinds[0], acc, gc.n), stage_c, acc, 0, 5, 1, rs_c)
+    rs = Scatter(at, ws, plans[1].rows, *outs[7:10], es.take(own_kinds[1], acc, gs.n), stage_s, acc, BEHIND, 3, HOP, rs_s)
 
     def over(k, src, dst):
         return at.copy(src, dst, y_s.at[k], y_r.at[k], at.z, at.x, at.c, 1 - at.s)

time: 418 us -> 406 us (0.971)
  Pallas kernels: 405 us -> 395 us
    pallas_call x1, Pallas kernels: 405 us -> 395 us  [layer_call(): pl.pallas_call(functools.partial(layer_kernel, plans, line), out_shape=ou...]
where the time goes in v2:
time: 406 us; the launch traced here: 402 us
  Pallas kernels  395 us (97%)
  local copies, waits for them, and re-layouts  6.54 us (2%)
    pallas_call x1, Pallas kernels, layer_call(): pl.pallas_call(functools.partial(layer_kernel, plans, line), out_shape=ou...  395 us

profile of v2, /device:TPU:9, one launch (start us, length us, event | category | flops | bytes accessed | tf_op | source)
XLA Modules:
  0.0 402.1 jit_solution(14289346567119908505)
XLA Ops:
  0.6 394.6 %layer.1 = (bf16[192,1024]{1,0:T(8,128)(2,1)}, f32[192,1024]{1,0:T(8,128)}, f32[4101,1,128]{2,1,0:T(1,128)}, f32[3461,1,128]{2,1,0:T(1,128)}, bf16[8,258,16,128]...) custom-call(s32[2]{0:T(128)} %texts.1, s32[2]{0:T(128)} %regions.1, ...), custom_call_target="tpu_custom_call" | custom-call | tf_op jit(solution)/shard_map/layer/pallas_call | solution.py:1459
  395.3 0.0 copy-start
  395.3 0.0 copy-start.1
  395.3 1.9 copy.14
  397.2 2.1 copy.15
  399.3 0.0 copy-done
  399.3 1.3 copy.16
  400.6 0.0 copy-done.1
  400.6 1.2 copy.17
Async XLA Ops:
  395.3 4.0 %copy-start = (f32[4101,1,128]{2,1,0:T(1,128)S(1)}, f32[4101,1,128]{2,1,0:T(1,128)}, u32[]{:S(2)}) copy-start(f32[4101,1,128]{2,1,0:T(1,128)} %get-tuple-element.10) | copy-start | bytes 6299140
  395.3 5.3 %copy-start.1 = (f32[3461,1,128]{2,1,0:T(1,128)S(1)}, f32[3461,1,128]{2,1,0:T(1,128)}, u32[]{:S(2)}) copy-start(f32[3461,1,128]{2,1,0:T(1,128)} %get-tuple-element.11) | copy-start | bytes 5316100

commit v3 on v2

--- a/solution.py
+++ b/solution.py
@@ -1114,7 +1114,7 @@
     ec, es = edges
     own_kinds = [[k[i] for k in kinds] for i in range(2)]
     rc = Scatter(at, wc, plans[0].rows, *outs[4:7], ec.take(own_kinds[0], acc, gc.n), stage_c, acc, 0, 5, 1, rs_c)
-    rs = Scatter(at, ws, plans[1].rows, *outs[7:10], es.take(own_kinds[1], acc, gs.n), stage_s, acc, BEHIND, 3, HOP, rs_s)
+    rs = Scatter(at, ws, plans[1].rows, *outs[7:10], es.take(own_kinds[1], acc, gs.n), stage_s, acc, BEHIND, 4, HOP, rs_s)
 
     def over(k, src, dst):
         return at.copy(src, dst, y_s.at[k], y_r.at[k], at.z, at.x, at.c, 1 - at.s)

time: 406 us -> 403 us (level)
  no operation moved by 1% of the time
where the time goes in v3:
time: 403 us; the launch traced here: 398 us
  Pallas kernels  391 us (97%)
  local copies, waits for them, and re-layouts  6.54 us (2%)
    pallas_call x1, Pallas kernels, layer_call(): pl.pallas_call(functools.partial(layer_kernel, plans, line), out_shape=ou...  391 us

profile of v3, /device:TPU:9, one launch (start us, length us, event | category | flops | bytes accessed | tf_op | source)
XLA Modules:
  0.0 398.5 jit_solution(6701626106470342562)
XLA Ops:
  0.6 391.1 %layer.1 = (bf16[192,1024]{1,0:T(8,128)(2,1)}, f32[192,1024]{1,0:T(8,128)}, f32[4101,1,128]{2,1,0:T(1,128)}, f32[3461,1,128]{2,1,0:T(1,128)}, bf16[8,258,16,128]...) custom-call(s32[2]{0:T(128)} %texts.1, s32[2]{0:T(128)} %regions.1, ...), custom_call_target="tpu_custom_call" | custom-call | tf_op jit(solution)/shard_map/layer/pallas_call | solution.py:1459
  391.7 0.0 copy-start
  391.7 0.0 copy-start.1
  391.7 1.9 copy.14
  393.6 2.1 copy.15
  395.7 0.0 copy-done
  395.7 1.3 copy.16
  397.0 0.0 copy-done.1
  397.0 1.2 copy.17
Async XLA Ops:
  391.7 4.0 %copy-start = (f32[4101,1,128]{2,1,0:T(1,128)S(1)}, f32[4101,1,128]{2,1,0:T(1,128)}, u32[]{:S(2)}) copy-start(f32[4101,1,128]{2,1,0:T(1,128)} %get-tuple-element.10) | copy-start | bytes 6299140
  391.7 5.3 %copy-start.1 = (f32[3461,1,128]{2,1,0:T(1,128)S(1)}, f32[3461,1,128]{2,1,0:T(1,128)}, u32[]{:S(2)}) copy-start(f32[3461,1,128]{2,1,0:T(1,128)} %get-tuple-element.11) | copy-start | bytes 5316100
